TPU v7x, 32 devices: a whole 2x2x4 slice. The times are simulated.
32 devices in a mesh: dp: 8 (over z, y), fsdp: 4 (over x, core).
Axes of the slice: x: 2, y: 2, z: 4, core: 2. Of those that a mesh axis runs over, the one named last changes fastest.
Arguments:
- tokens: bfloat16 [12288, 1024], P(('dp', 'fsdp')), may hold values from -6 to 6
- grad_out: bfloat16 [12288, 1024], P(('dp', 'fsdp')), may hold values from -6 to 6
- image_lengths: int32 [64], replicated, may hold values from 50 to 145, as said below
- image_device: int32 [64], replicated, may hold values from 0 to 31, as said below
- small_map: int32 [50], replicated, may hold values from 0 to 144, as said below
- ln1_gain: bfloat16 [1024], P(('dp', 'fsdp')), may hold values from 0.5 to 1.5
- ln1_bias: bfloat16 [1024], P(('dp', 'fsdp')), may hold values from -2 to 2
- qkv_weight: bfloat16 [1024, 3072], P(('dp', 'fsdp')), may hold values from -0.1875 to 0.1875
- q_bias: bfloat16 [1024], P(('dp', 'fsdp')), may hold values from -2 to 2
- v_bias: bfloat16 [1024], P(('dp', 'fsdp')), may hold values from -2 to 2
- out_weight: bfloat16 [1024, 1024], P(('dp', 'fsdp')), may hold values from -0.75 to 0.75
- out_bias: bfloat16 [1024], P(('dp', 'fsdp')), may hold values from -2 to 2
- ln2_gain: bfloat16 [1024], P(('dp', 'fsdp')), may hold values from 0.5 to 1.5
- ln2_bias: bfloat16 [1024], P(('dp', 'fsdp')), may hold values from -2 to 2
- up_weight: bfloat16 [1024, 4096], P(('dp', 'fsdp')), may hold values from -0.1875 to 0.1875
- up_bias: bfloat16 [4096], P(('dp', 'fsdp')), may hold values from -2 to 2
- down_weight: bfloat16 [4096, 1024], P(('dp', 'fsdp')), may hold values from -0.09375 to 0.09375
- down_bias: bfloat16 [1024], P(('dp', 'fsdp')), may hold values from -2 to 2
- pos_table: bfloat16 [145, 1024], P(None, ('dp', 'fsdp')), may hold values from -3 to 3
Outputs:
- layer_out: bfloat16 [12288, 1024], P(('dp', 'fsdp'))
- tokens_grad: bfloat16 [12288, 1024], P(('dp', 'fsdp'))
- ln1_gain_grad: float32 [1024], P(('dp', 'fsdp'))
- ln1_bias_grad: float32 [1024], P(('dp', 'fsdp'))
- qkv_weight_grad: float32 [1024, 3072], P(('dp', 'fsdp'))
- q_bias_grad: float32 [1024], P(('dp', 'fsdp'))
- v_bias_grad: float32 [1024], P(('dp', 'fsdp'))
- out_weight_grad: float32 [1024, 1024], P(('dp', 'fsdp'))
- out_bias_grad: float32 [1024], P(('dp', 'fsdp'))
- ln2_gain_grad: float32 [1024], P(('dp', 'fsdp'))
- ln2_bias_grad: float32 [1024], P(('dp', 'fsdp'))
- up_weight_grad: float32 [1024, 4096], P(('dp', 'fsdp'))
- up_bias_grad: float32 [4096], P(('dp', 'fsdp'))
- down_weight_grad: float32 [4096, 1024], P(('dp', 'fsdp'))
- down_bias_grad: float32 [1024], P(('dp', 'fsdp'))
- pos_table_grad: float32 [145, 1024], P(None, ('dp', 'fsdp'))
Inputs may be any that keep to these rules, and one draw needn't show every extreme that they name: `image_lengths`: each image has 50 or 145 tokens; both occur. `image_device`: every device block holds exactly 2 images. `small_map`: entry 0 is 0, the class token's row.
All inputs are finite; a program needn't handle non-finite values.
Results may differ from a plain program's by a relative error of at most 0.013.
Values may be sent and summed in bfloat16 or wider, within the bound.
No kernel may reach another device: no remote copies, remote signals or barrier semaphores. Data moves between devices by JAX's collectives and lax.ppermute only.
A program may use at most 192 MiB of HBM per device.

v0:
```python
import jax
import jax.numpy as jnp
from jax import lax
from jax.sharding import PartitionSpec as P

D = 1024
HEADS = 16
HEAD = 64
FF = 4096
LONG = 145
SHORT = 50


EPS = 1e-06


def fetch(parts):
    whole = (
        lax.all_gather(parts[0], ("dp", "fsdp"), axis=1, tiled=True),
        lax.all_gather(parts[1], ("dp", "fsdp"), axis=0, tiled=True),
        lax.all_gather(parts[2], ("dp", "fsdp"), axis=0, tiled=True),
        lax.all_gather(parts[3], ("dp", "fsdp"), axis=0, tiled=True),
        lax.all_gather(parts[4], ("dp", "fsdp"), axis=0, tiled=True),
        lax.all_gather(parts[5], ("dp", "fsdp"), axis=0, tiled=True),
        lax.all_gather(parts[6], ("dp", "fsdp"), axis=1, tiled=True),
    )
    return whole


def reduce_grads(parts):
    owned = (
        lax.psum_scatter(parts[0], ("dp", "fsdp"), scatter_dimension=1, tiled=True),
        lax.psum_scatter(parts[1], ("dp", "fsdp"), scatter_dimension=0, tiled=True),
        lax.psum_scatter(parts[2], ("dp", "fsdp"), scatter_dimension=0, tiled=True),
        lax.psum_scatter(parts[3], ("dp", "fsdp"), scatter_dimension=0, tiled=True),
        lax.psum_scatter(parts[4], ("dp", "fsdp"), scatter_dimension=0, tiled=True),
        lax.psum_scatter(parts[5], ("dp", "fsdp"), scatter_dimension=0, tiled=True),
        lax.psum_scatter(parts[6], ("dp", "fsdp"), scatter_dimension=1, tiled=True),
    )
    return owned


def layout(image_lengths, image_device, small_map, device, rows_dev):
    mine = image_device == device
    lens = jnp.where(mine, image_lengths, 0)
    starts = jnp.cumsum(lens) - lens
    rows = jnp.arange(rows_dev, dtype=jnp.int32)
    inside = (
        mine[None, :]
        & (starts[None, :] <= rows[:, None])
        & (rows[:, None] < (starts + lens)[None, :])
    )
    number = jnp.arange(image_lengths.shape[0], dtype=jnp.int32)
    segment = jnp.sum(jnp.where(inside, number[None, :] + 1, 0), axis=1) - 1
    offset = rows - jnp.sum(jnp.where(inside, starts[None, :], 0), axis=1)
    length = jnp.sum(jnp.where(inside, lens[None, :], 0), axis=1)
    spots = jnp.arange(SHORT, dtype=jnp.int32)
    mapped = jnp.sum(jnp.where(offset[:, None] == spots[None, :], small_map[None, :], 0), axis=1)
    place = jnp.where(length == LONG, offset, jnp.where(length == SHORT, mapped, 0))
    return (segment, place)


def layer_norm_forward_pass(v, norm_gain, shift_bias):
    centred_rows = v - jnp.mean(v, axis=1, keepdims=True)
    inverse_deviation = lax.rsqrt(
        jnp.mean(centred_rows * centred_rows, axis=1, keepdims=True) + EPS
    )
    normalized_rows = centred_rows * inverse_deviation
    return (normalized_rows * norm_gain + shift_bias, normalized_rows, inverse_deviation)


def layer_norm_backward_pass(upstream_gradient, normalized_rows, inverse_deviation, norm_gain):
    normalized_gradient = upstream_gradient * norm_gain
    first_input = jnp.mean(normalized_gradient, axis=1, keepdims=True)
    second_input = jnp.mean(normalized_gradient * normalized_rows, axis=1, keepdims=True)
    return (
        inverse_deviation * (normalized_gradient - first_input - normalized_rows * second_input),
        jnp.sum(upstream_gradient * normalized_rows, axis=0),
        jnp.sum(upstream_gradient, axis=0),
    )


def split_heads(values, groups):
    return values.reshape(values.shape[0], groups, HEADS // groups, HEAD).transpose(1, 0, 2, 3)


def join_heads(values):
    return values.transpose(1, 0, 2, 3).reshape(values.shape[1], D)


def masked_scores(query, keys, same):
    scores = jnp.einsum("thd,shd->hts", query, keys, preferred_element_type=jnp.float32) * HEAD ** (
        -0.5
    )
    return jnp.where(same[None], scores, -1000000000.0)


def attend_forward(qkvb, same):
    groups = HEADS // 4
    query = split_heads(qkvb[:, :D], groups)
    keys = split_heads(qkvb[:, D : 2 * D], groups)
    values = split_heads(qkvb[:, 2 * D :], groups)

    def one_group(item):
        scores = masked_scores(item[0], item[1], same)
        top = jnp.max(scores, axis=2, keepdims=True)
        lse = top + jnp.log(jnp.sum(jnp.exp(scores - top), axis=2, keepdims=True))
        probs = jnp.exp(scores - lse).astype(jnp.bfloat16)
        attended = jnp.einsum("hts,shd->thd", probs, item[2], preferred_element_type=jnp.float32)
        return (attended, lse[:, :, 0])

    attended, lse = lax.map(one_group, (query, keys, values))
    return (join_heads(attended), lse)


def attend_backward(qkvb, dob, lse, same):
    groups = HEADS // 4
    query = split_heads(qkvb[:, :D], groups)
    keys = split_heads(qkvb[:, D : 2 * D], groups)
    values = split_heads(qkvb[:, 2 * D :], groups)
    douts = split_heads(dob, groups)

    def one_group(item):
        scores = masked_scores(item[0], item[1], same)
        probs = jnp.exp(scores - item[4][:, :, None])
        dvalue = jnp.einsum(
            "hts,thd->shd", probs.astype(jnp.bfloat16), item[3], preferred_element_type=jnp.float32
        )
        dprobs = jnp.einsum("thd,shd->hts", item[3], item[2], preferred_element_type=jnp.float32)
        inner = jnp.sum(probs * dprobs, axis=2, keepdims=True)
        dscore = (probs * (dprobs - inner)).astype(jnp.bfloat16)
        dquery = jnp.einsum(
            "hts,shd->thd", dscore, item[1], preferred_element_type=jnp.float32
        ) * HEAD ** (-0.5)
        dkey = jnp.einsum(
            "hts,thd->shd", dscore, item[0], preferred_element_type=jnp.float32
        ) * HEAD ** (-0.5)
        return (dquery, dkey, dvalue)

    dquery, dkey, dvalue = lax.map(one_group, (query, keys, values, douts, lse))
    return jnp.concatenate([join_heads(dquery), join_heads(dkey), join_heads(dvalue)], axis=1)


def gelu_slope(x):
    return (
        0.5 * (1.0 + jax.scipy.special.erf(x * 0.7071067811865476))
        + x * jnp.exp(-0.5 * x * x) * 0.3989422804014327
    )


def on_device(
    tokens,
    grad_out,
    image_lengths,
    image_device,
    small_map,
    ln1_gain,
    ln1_bias,
    qkv_weight,
    q_bias,
    v_bias,
    out_weight,
    out_bias,
    ln2_gain,
    ln2_bias,
    up_weight,
    up_bias,
    down_weight,
    down_bias,
    pos_table,
):
    rows_dev = tokens.shape[0]
    device = lax.axis_index("dp") * lax.axis_size("fsdp") + lax.axis_index("fsdp")
    segment, place = layout(image_lengths, image_device, small_map, device, rows_dev)
    same = segment[:, None] == segment[None, :]
    valid = (segment >= 0).astype(jnp.float32)[:, None]
    table_rows = jnp.arange(LONG, dtype=jnp.int32)
    picker = place[:, None] == table_rows[None, :]
    vectors = jnp.stack(
        [ln1_gain, ln1_bias, q_bias, v_bias, out_bias, ln2_gain, ln2_bias, down_bias]
    )
    shards = (vectors, qkv_weight, out_weight, up_weight, up_bias, down_weight, pos_table)
    whole = fetch(shards)
    vec = whole[0].astype(jnp.float32)
    first_gain, first_centred, bq, bv, bo, second_gain, second_centred, bf2 = (
        vec[0],
        vec[1],
        vec[2],
        vec[3],
        vec[4],
        vec[5],
        vec[6],
        vec[7],
    )
    bf1 = whole[4].astype(jnp.float32)
    activation_rows = tokens.astype(jnp.float32) + jnp.dot(
        picker.astype(jnp.bfloat16), whole[6], preferred_element_type=jnp.float32
    )
    first_normed, first_normalized, first_inverse_deviation = layer_norm_forward_pass(
        activation_rows, first_gain, first_centred
    )
    n1b = first_normed.astype(jnp.bfloat16)
    bias3 = jnp.concatenate([bq, jnp.zeros_like(bq), bv])
    qkvb = (jnp.dot(n1b, whole[1], preferred_element_type=jnp.float32) + bias3).astype(jnp.bfloat16)
    attended, lse = attend_forward(qkvb, same)
    ob = attended.astype(jnp.bfloat16)
    second_activation = (
        activation_rows + jnp.dot(ob, whole[2], preferred_element_type=jnp.float32) + bo
    )
    second_normed, second_normalized, second_inverse_deviation = layer_norm_forward_pass(
        second_activation, second_gain, second_centred
    )
    n2b = second_normed.astype(jnp.bfloat16)
    hpre = jnp.dot(n2b, whole[3], preferred_element_type=jnp.float32) + bf1
    actb = jax.nn.gelu(hpre, approximate=False).astype(jnp.bfloat16)
    output = second_activation + jnp.dot(actb, whole[5], preferred_element_type=jnp.float32) + bf2
    layer_out = output.astype(jnp.bfloat16)
    dy = grad_out.astype(jnp.float32) * valid
    fenced, dy = lax.optimization_barrier((shards, dy))
    back = fetch(fenced)
    dyb = dy.astype(jnp.bfloat16)
    d_down = jnp.einsum("tf,td->fd", actb, dyb, preferred_element_type=jnp.float32)
    d_down_bias = jnp.sum(dy, axis=0)
    dgate = jnp.einsum("td,fd->tf", dyb, back[5], preferred_element_type=jnp.float32)
    dhb = (dgate * gelu_slope(hpre)).astype(jnp.bfloat16)
    d_up = jnp.einsum("td,tf->df", n2b, dhb, preferred_element_type=jnp.float32)
    d_up_bias = jnp.sum(dhb.astype(jnp.float32), axis=0)
    second_norm_gradient = jnp.einsum("tf,df->td", dhb, back[3], preferred_element_type=jnp.float32)
    second_activation_norm_gradient, second_gain_gradient, second_centred_gradient = (
        layer_norm_backward_pass(
            second_norm_gradient, second_normalized, second_inverse_deviation, second_gain
        )
    )
    da2 = dy + second_activation_norm_gradient
    dzb = da2.astype(jnp.bfloat16)
    d_out = jnp.einsum("te,td->ed", ob, dzb, preferred_element_type=jnp.float32)
    d_out_bias = jnp.sum(dzb.astype(jnp.float32), axis=0)
    dob = jnp.einsum("td,ed->te", dzb, back[2], preferred_element_type=jnp.float32).astype(
        jnp.bfloat16
    )
    dqkvb = attend_backward(qkvb, dob, lse, same).astype(jnp.bfloat16)
    d_qkv = jnp.einsum("td,te->de", n1b, dqkvb, preferred_element_type=jnp.float32)
    dqkv_sum = jnp.sum(dqkvb.astype(jnp.float32), axis=0)
    first_norm_gradient = jnp.einsum(
        "te,de->td", dqkvb, back[1], preferred_element_type=jnp.float32
    )
    first_activation_gradient, first_gain_gradient, first_centred_gradient = (
        layer_norm_backward_pass(
            first_norm_gradient, first_normalized, first_inverse_deviation, first_gain
        )
    )
    da = da2 + first_activation_gradient
    tokens_grad = da.astype(jnp.bfloat16)
    d_pos = jnp.dot(picker.astype(jnp.float32).T, da, precision=lax.Precision.HIGHEST)
    d_vectors = jnp.stack(
        [
            first_gain_gradient,
            first_centred_gradient,
            dqkv_sum[:D],
            dqkv_sum[2 * D :],
            d_out_bias,
            second_gain_gradient,
            second_centred_gradient,
            d_down_bias,
        ]
    )
    flat_parts = (
        d_vectors,
        d_qkv.reshape(-1, 128),
        d_out.reshape(-1, 128),
        d_up.reshape(-1, 128),
        d_up_bias,
        d_down,
        d_pos,
    )
    owned = reduce_grads(flat_parts)
    gv = owned[0]
    qkv_owned = owned[1].reshape(-1, 3 * D)
    out_owned = owned[2].reshape(-1, D)
    up_owned = owned[3].reshape(-1, FF)
    return (
        layer_out,
        tokens_grad,
        gv[0],
        gv[1],
        qkv_owned,
        gv[2],
        gv[3],
        out_owned,
        gv[4],
        gv[5],
        gv[6],
        up_owned,
        owned[4],
        owned[5],
        gv[7],
        owned[6],
    )


def solution(mesh):
    in_specs = (
        P(("dp", "fsdp"), None),
        P(("dp", "fsdp"), None),
        P(),
        P(),
        P(),
        P(("dp", "fsdp")),
        P(("dp", "fsdp")),
        P(("dp", "fsdp"), None),
        P(("dp", "fsdp")),
        P(("dp", "fsdp")),
        P(("dp", "fsdp"), None),
        P(("dp", "fsdp")),
        P(("dp", "fsdp")),
        P(("dp", "fsdp")),
        P(("dp", "fsdp"), None),
        P(("dp", "fsdp")),
        P(("dp", "fsdp"), None),
        P(("dp", "fsdp")),
        P(None, ("dp", "fsdp")),
    )
    out_specs = (
        P(("dp", "fsdp"), None),
        P(("dp", "fsdp"), None),
        P(("dp", "fsdp")),
        P(("dp", "fsdp")),
        P(("dp", "fsdp"), None),
        P(("dp", "fsdp")),
        P(("dp", "fsdp")),
        P(("dp", "fsdp"), None),
        P(("dp", "fsdp")),
        P(("dp", "fsdp")),
        P(("dp", "fsdp")),
        P(("dp", "fsdp"), None),
        P(("dp", "fsdp")),
        P(("dp", "fsdp"), None),
        P(("dp", "fsdp")),
        P(None, ("dp", "fsdp")),
    )
    return jax.shard_map(
        on_device, mesh=mesh, in_specs=in_specs, out_specs=out_specs, check_vma=False
    )
```

profile of v0, /device:TPU:0, one launch (start us, length us, event | category | flops | bytes accessed | tf_op | source)
XLA Modules:
  0.0 1532.4 jit_solution(12451901436736836609)
XLA Ops:
  16.7 44.9 %all_gather.33 = bf16[145,1024]{0,1:T(8,128)(2,1)S(1)} all-gather(bf16[145,32]{0,1:T(8,128)(2,1)S(1)} %copy-done.17), channel_id=1, replica_groups=mesh['dp'=8,'fsdp'=4] {'dp','fsdp'}, dimensions={1}, use_global_device_ids=true | all-gather | bytes 306240 | tf_op jit(solution)/shard_map/all_gather | solution.py:25
  61.6 36.6 %all-gather.1 = bf16[32,1,128]{2,1,0:T(2,128)(2,1)S(1)} all-gather(bf16[1,1,128]{2,1,0:T(2,128)(2,1)S(1)} %bitcast.238), channel_id=1, replica_groups=mesh['dp'=8,'fsdp'=4] {'dp','fsdp'}, dimensions={0}, use_global_device_ids=true | all-gather | bytes 8448 | tf_op jit(solution)/shard_map/all_gather | solution.py:23
  98.2 38.3 %all-gather = bf16[32,32,8]{1,2,0:T(8,128)(2,1)S(1)} all-gather(bf16[1,32,8]{1,2,0:T(8,128)(2,1)S(1)} %bitcast.223), channel_id=1, replica_groups=mesh['dp'=8,'fsdp'=4] {'dp','fsdp'}, dimensions={0}, use_global_device_ids=true | all-gather | bytes 16896 | tf_op jit(solution)/shard_map/all_gather | solution.py:19
  138.3 5.9 add_convert_fusion
  150.7 15.7 %while.28 = (s32[]{:T(128)}, bf16[4,384,4,64]{1,3,2,0:T(8,128)(2,1)}, f32[4,4,384]{2,1,0:T(4,128)S(1)}, bf16[4,384,4,64]{1,3,2,0:T(8,128)(2,1)}, bf16[4,384,4,64...) while((s32[]{:T(128)}, ...), condition=%wide.region_10.11_spmd.clone, body=%wide.region_7.10_spmd.clone.sunk | while | flops 157628928 | bytes 14995097 | solution.py:112
  170.9 50.9 %all-gather.15.cloned.1.call-done = bf16[1024,4096]{1,0:T(8,128)(2,1)} async-done(((bf16[32,4096]{1,0:T(8,128)(2,1)}), bf16[1024,4096]{1,0:T(8,128)(2,1)}) %all-gather.15.cloned.1.call-update) | async-done | bytes 8388624 | tf_op jit(solution)/shard_map/all_gather | solution.py:22
  221.8 21.1 %fusion.48 = (bf16[384,4096]{1,0:T(8,128)(2,1)}, f32[384,4096]{1,0:T(8,128)}) fusion(f32[4096]{0:T(1024)S(1)} %bitcast.215, bf16[1024,4096]{1,0:T(8,128)(2,1)} %all-gather.15.cloned.1.call-done, f32[384,1024]{1,0:T(8,128)S(1)} %get-tuple-element.245, f32[1024]{0:T(1024)S(1)} %bitcast.209, f32[1024]{0:T(1024)S(1)} %bitcast.205, f32[384]{0:T(512)S(1)} %add_rsqrt_fusion, ...), kind=kOutput, calls=%fused_computation.63 | convolution fusion | flops 3327000576 | bytes 19426304 | tf_op jit(solution)/shard_map/dot_general | solution.py:214
  242.9 57.7 %all-gather.19.cloned.1.call-done = bf16[4096,1024]{1,0:T(8,128)(2,1)} async-done(((bf16[128,1024]{1,0:T(8,128)(2,1)}), bf16[4096,1024]{1,0:T(8,128)(2,1)}) %all-gather.19.cloned.1.call-update) | async-done | bytes 8388624 | tf_op jit(solution)/shard_map/all_gather | solution.py:24
  300.5 10.1 convert_reduce_fusion
  310.7 68.6 %all-gather.21.cloned.1.call-done = bf16[1024,4096]{1,0:T(8,128)(2,1)} async-done(((bf16[32,4096]{1,0:T(8,128)(2,1)}), bf16[1024,4096]{1,0:T(8,128)(2,1)}) %all-gather.21.cloned.1.call-update) | async-done | bytes 8388624 | tf_op jit(solution)/shard_map/all_gather | solution.py:22
  379.3 7.6 multiply_reduce_fusion.1
  388.8 48.2 %all-gather.23.cloned.1.call-done = bf16[1024,1024]{1,0:T(8,128)(2,1)} async-done(((bf16[32,1024]{1,0:T(8,128)(2,1)}), bf16[1024,1024]{1,0:T(8,128)(2,1)}) %all-gather.23.cloned.1.call-update) | async-done | bytes 2097168 | tf_op jit(solution)/shard_map/all_gather | solution.py:21
  437.0 4.0 convolution_convert_fusion
  446.3 31.3 %while.29 = (s32[]{:T(128)}, bf16[4,384,4,64]{1,3,2,0:T(8,128)(2,1)}, bf16[4,384,4,64]{1,3,2,0:T(8,128)(2,1)}, bf16[4,384,4,64]{1,3,2,0:T(8,128)(2,1)}, bf16[4,3...) while((s32[]{:T(128)}, ...), condition=%wide.region_17.18_spmd.clone, body=%wide.region_15.17_spmd.clone.sunk | while | flops 383138304 | bytes 45749080 | solution.py:140
  479.7 28.6 %all-gather.25.cloned.1.call-done = bf16[1024,3072]{1,0:T(8,128)(2,1)} async-done(((bf16[32,3072]{1,0:T(8,128)(2,1)}), bf16[1024,3072]{1,0:T(8,128)(2,1)}) %all-gather.25.cloned.1.call-update) | async-done | bytes 6291472 | tf_op jit(solution)/shard_map/all_gather | solution.py:20
  508.3 7.6 multiply_reduce_fusion.2
  517.0 4.9 fusion.70
  522.0 4.9 reshape.223
  526.9 8.7 fusion.73
  535.6 13.9 reshape.221
  549.5 10.9 fusion.75
  560.4 18.1 %reshape.225 = f32[32768,128]{1,0:T(8,128)} reshape(f32[1024,4096]{1,0:T(8,128)} %fusion.75) | data formatting | bytes 33554432 | tf_op jit(solution)/shard_map/reshape | solution.py:271
  578.6 3.3 fusion.77
  584.5 10.3 fusion.62
  594.8 39.7 %all-reduce = f32[4096]{0:T(1024)S(1)} all-reduce(f32[4096]{0:T(1024)S(1)} %get-tuple-element.250), channel_id=6, replica_groups=mesh['dp'=8,'fsdp'=4] {'dp','fsdp'}, use_global_device_ids=true, to_apply=%region_32.33.clone | all-reduce | flops 4096 | bytes 32768
  635.0 8.6 add_convert_fusion.1
  643.7 78.9 %reduce-scatter.19.cloned.1.call-done = f32[32,8]{1,0:T(8,128)} async-done(((f32[1024,8]{1,0:T(8,128)}), f32[32,8]{1,0:T(8,128)}) %reduce-scatter.19.cloned.1.call-update) | async-done | bytes 1040
  728.3 133.6 %reduce-scatter.11.cloned.1.call-done = f32[256,128]{1,0:T(8,128)} async-done(((f32[8192,128]{1,0:T(8,128)}), f32[256,128]{1,0:T(8,128)}) %reduce-scatter.11.cloned.1.call-update) | async-done | bytes 131088 | tf_op jit(solution)/shard_map/reduce_scatter | solution.py:34
  863.5 156.8 %reduce-scatter.9.cloned.1.call-done = f32[768,128]{1,0:T(8,128)} async-done(((f32[24576,128]{1,0:T(8,128)}), f32[768,128]{1,0:T(8,128)}) %reduce-scatter.9.cloned.1.call-update) | async-done | bytes 393232 | tf_op jit(solution)/shard_map/reduce_scatter | solution.py:33
  1022.1 182.2 %reduce-scatter.13.cloned.1.call-done = f32[1024,128]{1,0:T(8,128)} async-done(((f32[32768,128]{1,0:T(8,128)}), f32[1024,128]{1,0:T(8,128)}) %reduce-scatter.13.cloned.1.call-update) | async-done | bytes 524304 | tf_op jit(solution)/shard_map/reduce_scatter | solution.py:35
  1206.2 137.5 %reduce-scatter.17.cloned.1.call-done = f32[145,32]{0,1:T(8,128)} async-done(((f32[145,1024]{0,1:T(8,128)}), f32[145,32]{0,1:T(8,128)}) %reduce-scatter.17.cloned.1.call-update) | async-done | bytes 18576 | tf_op jit(solution)/shard_map/reduce_scatter | solution.py:38
  1343.7 181.7 %reduce-scatter.15.cloned.1.call-done = f32[128,1024]{1,0:T(8,128)} async-done(((f32[4096,1024]{1,0:T(8,128)}), f32[128,1024]{1,0:T(8,128)}) %reduce-scatter.15.cloned.1.call-update) | async-done | bytes 524304 | tf_op jit(solution)/shard_map/reduce_scatter | solution.py:37
  (245 shorter events, 93.1 us)
Async XLA Ops:
  7.2 9.5 copy-start.17
  7.2 54.4 %copy-start.19 = (bf16[128]{0:T(256)(128)(2,1)S(1)}, bf16[128]{0:T(256)(128)(2,1)}, u32[]{:S(2)}) copy-start(bf16[128]{0:T(256)(128)(2,1)} %param.38) | copy-start | bytes 772
  7.2 131.1 %all-gather.11.cloned.1.call-start = ((), (), s32[]{:S(2)}) async-start(), calls=%async_computation.6 | async-start | bytes 6488064 | tf_op jit(solution)/shard_map/all_gather | solution.py:20
  7.9 158.5 %all-gather.13.cloned.1.call-start = ((), (), s32[]{:S(2)}) async-start(), calls=%async_computation.7 | async-start | bytes 2162688 | tf_op jit(solution)/shard_map/all_gather | solution.py:21
  8.7 213.1 %all-gather.15.cloned.1.call-start = ((), (), s32[]{:S(2)}) async-start(), calls=%async_computation.8 | async-start | bytes 8650752 | tf_op jit(solution)/shard_map/all_gather | solution.py:22
  9.4 127.9 %copy-start.20 = (s32[50]{0:T(128)S(1)}, s32[50]{0:T(128)}, u32[]{:S(2)}) copy-start(s32[50]{0:T(128)} %param.27) | copy-start | bytes 604
  9.4 291.1 %all-gather.19.cloned.1.call-start = ((), (), s32[]{:S(2)}) async-start(), calls=%async_computation.10 | async-start | bytes 8650752 | tf_op jit(solution)/shard_map/all_gather | solution.py:24
  9.5 127.9 %copy-start.14 = (bf16[384,1024]{1,0:T(8,128)(2,1)S(1)}, bf16[384,1024]{1,0:T(8,128)(2,1)}, u32[]{:S(2)}) copy-start(bf16[384,1024]{1,0:T(8,128)(2,1)} %param.23) | copy-start | bytes 2359300
  14.0 365.3 %all-gather.21.cloned.1.call-start = ((), (), s32[]{:S(2)}) async-start(), calls=%async_computation.11 | async-start | bytes 8650752 | tf_op jit(solution)/shard_map/all_gather | solution.py:22
  14.6 422.4 %all-gather.23.cloned.1.call-start = ((), (), s32[]{:S(2)}) async-start(), calls=%async_computation.12 | async-start | bytes 2162688 | tf_op jit(solution)/shard_map/all_gather | solution.py:21
  15.1 493.2 %all-gather.25.cloned.1.call-start = ((), (), s32[]{:S(2)}) async-start(), calls=%async_computation.13 | async-start | bytes 6488064 | tf_op jit(solution)/shard_map/all_gather | solution.py:20
  15.9 619.2 %all-gather.17.cloned.1.call-start = ((), (), s32[]{:S(2)}) async-start(), calls=%async_computation.9 | async-start | bytes 8650752 | tf_op jit(solution)/shard_map/all_gather | solution.py:24
  16.6 705.9 %reduce-scatter.19.cloned.1.call-start = ((), (), s32[]{:S(2)}) async-start(), calls=%async_computation.19 | async-start | bytes 540672
  137.4 6.8 copy-start.15
  379.3 7.6 copy-start.4
  446.3 1.8 copy-start.1
  446.3 1.8 copy-start.3
  450.2 2.2 copy-start.12
  454.1 1.8 copy-start.3
  458.0 2.2 copy-start.12
  462.0 1.8 copy-start.3
  465.8 2.2 copy-start.12
  469.8 1.8 copy-start.3
  473.7 2.2 copy-start.12
  517.0 344.9 %reduce-scatter.11.cloned.1.call-start = ((), (), s32[]{:S(2)}) async-start(), calls=%async_computation.15 | async-start | bytes 4325376 | tf_op jit(solution)/shard_map/reduce_scatter | solution.py:34
  526.9 493.4 %reduce-scatter.9.cloned.1.call-start = ((), (), s32[]{:S(2)}) async-start(), calls=%async_computation.14 | async-start | bytes 12976128 | tf_op jit(solution)/shard_map/reduce_scatter | solution.py:33
  549.5 654.8 %reduce-scatter.13.cloned.1.call-start = ((), (), s32[]{:S(2)}) async-start(), calls=%async_computation.16 | async-start | bytes 17301504 | tf_op jit(solution)/shard_map/reduce_scatter | solution.py:35
  578.5 765.2 %reduce-scatter.17.cloned.1.call-start = ((), (), s32[]{:S(2)}) async-start(), calls=%async_computation.18 | async-start | bytes 1081344 | tf_op jit(solution)/shard_map/reduce_scatter | solution.py:38
  578.6 3.3 copy-start.16
  581.9 2.6 copy-start.5
  584.4 941.0 %reduce-scatter.15.cloned.1.call-start = ((), (), s32[]{:S(2)}) async-start(), calls=%async_computation.17 | async-start | bytes 17301504 | tf_op jit(solution)/shard_map/reduce_scatter | solution.py:37
  594.8 40.3 %copy-start.18 = (f32[1,1024]{1,0:T(1,128)S(1)}, f32[1,1024]{1,0:T(1,128)}, u32[]{:S(2)}) copy-start(f32[1,1024]{1,0:T(1,128)} %get-tuple-element.224) | copy-start | bytes 12292
  (33 other events, 37.3 us)
Sparse Core Ops, SparseCore 0:
  10.9 73.7 all-gather.10
  87.5 54.9 all-gather.12
  145.4 76.2 all-gather.14
  224.5 76.0 all-gather.18
  303.3 75.9 all-gather.20
  382.0 54.9 all-gather.22
  439.9 68.3 all-gather.24
  511.1 75.9 all-gather.16
  590.0 132.5 reduce-scatter.18
  724.8 137.1 reduce-scatter.10
  869.0 151.2 reduce-scatter.8
  1022.4 181.7 reduce-scatter.12
  1207.1 136.5 reduce-scatter.16
  1346.5 178.8 reduce-scatter.14
where the time goes:
time: 1540 us; the launch traced here: 1530 us
  waiting for transfers between devices  1130 us (73%)
  blocking collectives  159 us (10%)
  matrix products  135 us (9%)
  local copies, waits for them, and re-layouts  76.6 us (5%)
  other arithmetic  16.2 us (1%)
    reduce_scatter x1, waiting for transfers between devices, reduce_grads(): lax.psum_scatter(parts[3], ('dp', 'fsdp'), scatter_dimension=0, tiled=True)  182 us
    reduce_scatter x1, waiting for transfers between devices, reduce_grads(): lax.psum_scatter(parts[5], ('dp', 'fsdp'), scatter_dimension=0, tiled=True)  182 us
    reduce_scatter x1, waiting for transfers between devices, reduce_grads(): lax.psum_scatter(parts[1], ('dp', 'fsdp'), scatter_dimension=0, tiled=True)  157 us
    reduce_scatter x1, waiting for transfers between devices, reduce_grads(): lax.psum_scatter(parts[6], ('dp', 'fsdp'), scatter_dimension=1, tiled=True)  137 us
    reduce_scatter x1, waiting for transfers between devices, reduce_grads(): lax.psum_scatter(parts[2], ('dp', 'fsdp'), scatter_dimension=0, tiled=True)  134 us
    all_gather x2, waiting for transfers between devices, fetch(): lax.all_gather(parts[3], ('dp', 'fsdp'), axis=0, tiled=True)  120 us
    unnamed x15, waiting for transfers between devices  83.5 us
    all_gather x2, waiting for transfers between devices, fetch(): lax.all_gather(parts[5], ('dp', 'fsdp'), axis=0, tiled=True)  57.7 us
  transfers between devices with their start and end apart: 14, of which 11 were waited for; matrix products, arithmetic and copies ran while one was open for 14% of the time, Pallas kernels for 0%

commit v1 on v0

--- a/solution.py
+++ b/solution.py
@@ -1,6 +1,9 @@
 import jax
 import jax.numpy as jnp
+import numpy as np
 from jax import lax
+from jax.experimental import pallas as pl
+from jax.experimental.pallas import tpu as pltpu
 from jax.sharding import PartitionSpec as P
 
 D = 1024
@@ -298,6 +301,504 @@
     )
 
 
+BF = jnp.bfloat16
+F32 = jnp.float32
+AXES = ("dp", "fsdp")
+CORE, XBIT, YBIT, ZBIT = 1, 2, 4, 8
+
+
+def swap(value, mask):
+    return lax.ppermute(value, AXES, [(i, i ^ mask) for i in range(32)])
+
+
+def coords():
+    dp = lax.axis_index("dp")
+    fs = lax.axis_index("fsdp")
+    return dp // 2, dp % 2, fs // 2, fs % 2
+
+
+def chip_of(rel):
+    z, y, x, _ = coords()
+    dz, dy, dx = rel
+    bits = 0
+    for part, off, width in ((z // 2, dz // 2, 8), (z % 2, dz % 2, 4), (y, dy, 2), (x, dx, 1)):
+        bits = bits + (1 - part if off else part) * width
+    return bits
+
+
+ENTRIES_ZXY = (
+    [(0, (k,), h, (k, 0, 0), h) for k in range(4) for h in range(2)]
+    + [(1, (k,), h, (k, 0, 1), h) for k in range(4) for h in range(2)]
+    + [(2, (k,), h, (k, 1, 0), h) for k in range(4) for h in range(2)]
+    + [(3, (k,), h, (k, 1, 1), h) for k in range(2) for h in range(2)]
+    + [(4, (k,), h, (k + 2, 1, 1), h) for k in range(2) for h in range(2)]
+)
+QUADS = (((0, 0), 0), ((0, 1), 0), ((0, 0), 1), ((1, 0), 1))
+SIDE_A = ((1, 0), (1, 1))
+SIDE_B = ((0, 1), (1, 1))
+ENTRIES_XZY_GATHER = (
+    [(k, (q,), 0, (k,) + QUADS[q][0], QUADS[q][1]) for k in range(4) for q in range(4)]
+    + [(4, (k, q), 0, (k,) + SIDE_A[q], 0) for k in range(4) for q in range(2)]
+    + [(5, (k, q), 0, (k,) + SIDE_B[q], 1) for k in range(4) for q in range(2)]
+)
+ENTRIES_XZY_SCATTER = (
+    [(0, (k, q), 0, (k,) + QUADS[q][0], QUADS[q][1]) for k in range(4) for q in range(4)]
+    + [(1, (k, q), 0, (k,) + SIDE_A[q], 0) for k in range(4) for q in range(2)]
+    + [(2, (k, q), 0, (k,) + SIDE_B[q], 1) for k in range(4) for q in range(2)]
+)
+
+
+def gather_zxy(block):
+    line = jnp.stack([block] + [swap(block, ZBIT * k) for k in range(1, 4)])
+    from_x = swap(line, XBIT)
+    from_y = swap(line, YBIT)
+    corner_a = swap(from_x[:2], YBIT)
+    corner_b = swap(from_y[2:], XBIT)
+    return [line, from_x, from_y, corner_a, corner_b], ENTRIES_ZXY
+
+
+def gather_xzy(block):
+    half_a, half_b = block[:32], block[32:]
+    quad = jnp.stack([half_a, swap(half_a, XBIT), half_b, swap(half_b, YBIT)])
+    quads = [quad] + [swap(quad, ZBIT * k) for k in range(1, 4)]
+    side_a = swap(jnp.stack([q[:2] for q in quads]), YBIT)
+    side_b = swap(jnp.stack([q[2:] for q in quads]), XBIT)
+    return quads + [side_a, side_b], ENTRIES_XZY_GATHER
+
+
+def add(*values):
+    total = values[0].astype(F32)
+    for value in values[1:]:
+        total = total + value.astype(F32)
+    return total
+
+
+def scatter_zxy(parts):
+    line, to_x, to_y, corner_a, corner_b = parts
+    got_a = swap(corner_a, XBIT)
+    got_b = swap(corner_b, YBIT)
+    to_x = jnp.concatenate([to_x[:2], add(to_x[2:], got_b).astype(BF)])
+    to_y = jnp.concatenate([add(to_y[:2], got_a).astype(BF), to_y[2:]])
+    got_x = swap(to_x, XBIT)
+    got_y = swap(to_y, YBIT)
+    sums = [add(line[k], got_x[k], got_y[k]) for k in range(4)]
+    got_z = [swap(sums[k].astype(BF), ZBIT * k) for k in range(1, 4)]
+    return add(sums[0], *got_z)
+
+
+def scatter_xzy(parts):
+    keep, side_a, side_b = parts
+    got_a = swap(side_a, YBIT)
+    got_b = swap(side_b, XBIT)
+    quads = [add(keep[k], jnp.concatenate([got_a[k], got_b[k]])) for k in range(4)]
+    got_z = [swap(quads[k].astype(BF), ZBIT * k) for k in range(1, 4)]
+    quad = add(quads[0], *got_z)
+    got_x = swap(quad[1].astype(BF), XBIT)
+    got_y = swap(quad[3].astype(BF), YBIT)
+    return jnp.concatenate([add(quad[0], got_x), add(quad[2], got_y)])
+
+
+def shapes_for(kind, width):
+    if kind == "zxy":
+        return [(4, 64, width)] * 3 + [(2, 64, width)] * 2, ENTRIES_ZXY
+    return [(4, 4, 32, width), (4, 2, 32, width), (4, 2, 32, width)], ENTRIES_XZY_SCATTER
+
+
+def piece_of(ref, entry, lanes):
+    _, index, row, _, _ = entry
+    return ref.at[index + (pl.ds(32 * row, 32), pl.ds(*lanes))]
+
+
+def run_copies(copies, sems):
+    started = []
+    for i, (src, dst) in enumerate(copies):
+        copy = pltpu.make_async_copy(src, dst, sems.at[i])
+        copy.start()
+        started.append(copy)
+    for copy in started:
+        copy.wait()
+
+
+def mover(sources, out_shapes, plan, count, inward):
+    n_in, n_out = len(sources), len(out_shapes)
+
+    def kernel(*refs):
+        run_copies(plan(refs[:n_in], refs[n_in : n_in + n_out]), refs[-1])
+
+    size = sum(int(np.prod(s)) for s in out_shapes) * 2
+    return pl.pallas_call(
+        kernel,
+        out_shape=[jax.ShapeDtypeStruct(s, BF) for s in out_shapes],
+        in_specs=[pl.BlockSpec(memory_space=pl.ANY if inward else pltpu.VMEM)] * n_in,
+        out_specs=[pl.BlockSpec(memory_space=pltpu.VMEM if inward else pl.ANY)] * n_out,
+        scratch_shapes=[pltpu.SemaphoreType.DMA((count,))],
+        cost_estimate=pl.CostEstimate(flops=0, bytes_accessed=2 * size, transcendentals=0),
+        compiler_params=pltpu.CompilerParams(vmem_limit_bytes=24 << 20),
+    )(*sources)
+
+
+def rows_of(rel, half):
+    core = coords()[3]
+    side = core if half == 0 else 1 - core
+    return pl.multiple_of(chip_of(rel) * 64 + side * 32, 32)
+
+
+SMALL = 384
+QKV_OWN = 1536
+HALF_D = 512
+A_WIDTH = SMALL + QKV_OWN + HALF_D
+
+
+def places_a(small, qkv, out, entry):
+    rel, half = entry[3], entry[4]
+    row = rows_of(rel, half)
+    return [
+        ((0, SMALL), small.at[pl.ds(row, 32), :]),
+        ((SMALL, QKV_OWN), qkv.at[pl.ds(row, 32), :]),
+        (
+            (SMALL + QKV_OWN, HALF_D),
+            out.at[chip_of(rel), :, pl.ds(HALF_D * half, HALF_D)],
+        ),
+    ]
+
+
+def places_up(up, entry):
+    return [((0, 2048), up.at[pl.ds(rows_of(entry[3], entry[4]), 32), :])]
+
+
+def places_down(down, entry):
+    rel, half = entry[3], entry[4]
+    row = pl.multiple_of(chip_of(rel) * 128 + 32 * half, 32)
+    return [
+        ((0, D), down.at[pl.ds(row, 32), :]),
+        ((D, D), down.at[pl.ds(row + 64, 32), :]),
+    ]
+
+
+A_SHAPES = [(D, SMALL), (D, QKV_OWN), (16, 32, D)]
+
+
+def assemble(gathered, places, out_shapes):
+    arrays, entries = gathered
+
+    def plan(ins, outs):
+        copies = []
+        for entry in entries:
+            for lanes, dst in places(*outs, entry):
+                copies.append((piece_of(ins[entry[0]], entry, lanes), dst))
+        return copies
+
+    return mover(arrays, out_shapes, plan, len(entries) * 3, True)
+
+
+def disassemble(wholes, places, kind, width):
+    shapes, entries = shapes_for(kind, width)
+
+    def plan(ins, outs):
+        copies = []
+        for entry in entries:
+            for lanes, src in places(*ins, entry):
+                copies.append((src, piece_of(outs[entry[0]], entry, lanes)))
+        return copies
+
+    return mover(wholes, shapes, plan, len(entries) * 3, False)
+
+
+def softmax_parts(query, keys, same):
+    scores = lax.dot_general(query, keys, (((1,), (1,)), ((), ())), preferred_element_type=F32)
+    scores = jnp.where(same, scores * HEAD ** (-0.5), -1000000000.0)
+    top = jnp.max(scores, axis=1, keepdims=True)
+    powers = jnp.exp(scores - top)
+    return powers / jnp.sum(powers, axis=1, keepdims=True)
+
+
+def lane_masks(rows):
+    lane = lax.broadcasted_iota(jnp.int32, (rows, 128), 1)
+    return lane < 64
+
+
+def attend_kernel(q_ref, k_ref, v_ref, col_ref, row_ref, o_ref):
+    same = col_ref[...] == row_ref[0]
+    first = lane_masks(q_ref.shape[0])
+    q, k, v = q_ref[...], k_ref[...], v_ref[...]
+    zero = jnp.zeros_like(q)
+    outs = []
+    for h in range(2):
+        mask = first if h == 0 else ~first
+        probs = softmax_parts(jnp.where(mask, q, zero), k, same).astype(BF)
+        outs.append(jnp.dot(probs, v, preferred_element_type=F32))
+    o_ref[...] = jnp.where(first, outs[0], outs[1]).astype(BF)
+
+
+def attend_back_kernel(q_ref, k_ref, v_ref, g_ref, col_ref, row_ref, dq_ref, dk_ref, dv_ref):
+    same = col_ref[...] == row_ref[0]
+    first = lane_masks(q_ref.shape[0])
+    q, k, v, g = q_ref[...], k_ref[...], v_ref[...], g_ref[...]
+    zero = jnp.zeros_like(q)
+    dq, dk, dv = [], [], []
+    over_rows = (((0,), (0,)), ((), ()))
+    for h in range(2):
+        mask = first if h == 0 else ~first
+        probs = softmax_parts(jnp.where(mask, q, zero), k, same)
+        dv.append(lax.dot_general(probs.astype(BF), g, over_rows, preferred_element_type=F32))
+        dprobs = lax.dot_general(
+            jnp.where(mask, g, zero), v, (((1,), (1,)), ((), ())), preferred_element_type=F32
+        )
+        inner = jnp.sum(probs * dprobs, axis=1, keepdims=True)
+        ds = (probs * (dprobs - inner)).astype(BF)
+        dq.append(jnp.dot(ds, k, preferred_element_type=F32))
+        dk.append(lax.dot_general(ds, q, over_rows, preferred_element_type=F32))
+    scale = HEAD ** (-0.5)
+    dq_ref[...] = (jnp.where(first, dq[0], dq[1]) * scale).astype(BF)
+    dk_ref[...] = (jnp.where(first, dk[0], dk[1]) * scale).astype(BF)
+    dv_ref[...] = jnp.where(first, dv[0], dv[1]).astype(BF)
+
+
+def attend(qkv, seg):
+    rows = qkv.shape[0] // 2
+    col, row = seg[:, None], seg.reshape(2, 1, rows)
+    part = lambda off: pl.BlockSpec((rows, 128), lambda i, j: (i, j + off))
+    return pl.pallas_call(
+        attend_kernel,
+        grid=(2, 4),
+        in_specs=[
+            part(0),
+            part(4),
+            part(8),
+            pl.BlockSpec((rows, 1), lambda i, j: (i, 0)),
+            pl.BlockSpec((1, 1, rows), lambda i, j: (i, 0, 0)),
+        ],
+        out_specs=part(0),
+        out_shape=jax.ShapeDtypeStruct((2 * rows, 512), BF),
+        cost_estimate=pl.CostEstimate(flops=int(1.5e9), bytes_accessed=4000000, transcendentals=2400000),
+        compiler_params=pltpu.CompilerParams(vmem_limit_bytes=40 << 20),
+    )(qkv, qkv, qkv, col, row)
+
+
+def attend_back(qkv, grad, seg):
+    rows = qkv.shape[0] // 2
+    col, row = seg[:, None], seg.reshape(2, 1, rows)
+    part = lambda off: pl.BlockSpec((rows, 128), lambda i, j: (i, j + off))
+    return pl.pallas_call(
+        attend_back_kernel,
+        grid=(2, 4),
+        in_specs=[
+            part(0),
+            part(4),
+            part(8),
+            part(0),
+            pl.BlockSpec((rows, 1), lambda i, j: (i, 0)),
+            pl.BlockSpec((1, 1, rows), lambda i, j: (i, 0, 0)),
+        ],
+        out_specs=[part(0)] * 3,
+        out_shape=[jax.ShapeDtypeStruct((2 * rows, 512), BF)] * 3,
+        cost_estimate=pl.CostEstimate(flops=int(3e9), bytes_accessed=6000000, transcendentals=2400000),
+        compiler_params=pltpu.CompilerParams(vmem_limit_bytes=40 << 20),
+    )(qkv, qkv, qkv, grad, col, row)
+
+
+def pick_blocks(value, which):
+    n = value.shape[1] // 256
+    even = jnp.concatenate([value[:, 256 * j : 256 * j + 128] for j in range(n)], axis=1)
+    odd = jnp.concatenate([value[:, 256 * j + 128 : 256 * j + 256] for j in range(n)], axis=1)
+    return jnp.where(which == 0, even, odd)
+
+
+def weave_blocks(own, other, core):
+    even = jnp.where(core == 0, own, other)
+    odd = jnp.where(core == 0, other, own)
+    n = own.shape[1] // 128
+    parts = []
+    for j in range(n):
+        parts += [even[:, 128 * j : 128 * (j + 1)], odd[:, 128 * j : 128 * (j + 1)]]
+    return jnp.concatenate(parts, axis=1)
+
+
+def swap_halves(value):
+    half = value.shape[0] // 2
+    return jnp.concatenate([value[half:], value[:half]])
+
+
+def fast_on_device(
+    tokens,
+    grad_out,
+    image_lengths,
+    image_device,
+    small_map,
+    ln1_gain,
+    ln1_bias,
+    qkv_weight,
+    q_bias,
+    v_bias,
+    out_weight,
+    out_bias,
+    ln2_gain,
+    ln2_bias,
+    up_weight,
+    up_bias,
+    down_weight,
+    down_bias,
+    pos_table,
+):
+    rows = tokens.shape[0]
+    core = coords()[3]
+    device = lax.axis_index("dp") * 4 + lax.axis_index("fsdp")
+    seg, place = layout(image_lengths, image_device, small_map, device, rows)
+    seg2, place2 = layout(image_lengths, image_device, small_map, device ^ 1, rows)
+    seg = jnp.concatenate([seg, seg2])
+    place = jnp.concatenate([place, place2])
+    valid = (seg >= 0).astype(F32)[:, None]
+    picker = place[:, None] == jnp.arange(256, dtype=jnp.int32)[None, :]
+
+    vectors = jnp.stack([ln1_gain, ln1_bias, q_bias, v_bias, out_bias, ln2_gain, ln2_bias, down_bias])
+    small = jnp.concatenate([pos_table, vectors, jnp.zeros((103, 32), BF)]).T
+    small = jnp.concatenate(
+        [small, jnp.concatenate([up_bias[None, :], jnp.zeros((31, 128), BF)])], axis=1
+    )
+    keep = jnp.concatenate([small, pick_blocks(qkv_weight, core), pick_blocks(up_weight, core)], axis=1)
+    send = jnp.concatenate(
+        [small, pick_blocks(qkv_weight, 1 - core), pick_blocks(up_weight, 1 - core)], axis=1
+    )
+    got = swap(send, CORE)
+    both = jnp.concatenate([keep, got])
+    toks = jnp.concatenate([tokens, swap(tokens, CORE)])
+    gout = jnp.concatenate([grad_out, swap(grad_out, CORE)])
+    cut = SMALL + QKV_OWN
+    out_part = jnp.concatenate([out_weight[:, :HALF_D], out_weight[:, HALF_D:]])
+    chunk_a = jnp.concatenate([both[:, :cut], out_part], axis=1)
+    chunk_u = both[:, cut:]
+    chunk_d = jnp.concatenate([down_weight[:64], down_weight[64:]], axis=1)
+
+    small_all, w_qkv, out_own = assemble(gather_zxy(chunk_a), places_a, A_SHAPES)
+    (w_up,) = assemble(gather_zxy(chunk_u), places_up, [(D, 2048)])
+    (w_down,) = assemble(gather_xzy(chunk_d), places_down, [(2048, D)])
+    out_other = swap(out_own, CORE)
+
+    def own_heads(value):
+        return lax.dynamic_index_in_dim(value.reshape(4, 2, 2, 32, D), core, 1, False)
+
+    mine, other = own_heads(out_own), own_heads(out_other)
+    w_out = jnp.concatenate(
+        [jnp.where(core == 0, mine, other), jnp.where(core == 0, other, mine)], axis=2
+    ).reshape(512, D)
+
+    vec = small_all[:, 145:153].T.astype(F32)
+    gain1, shift1, bq, bv, bo, gain2, shift2, bf2 = (vec[i] for i in range(8))
+    bf1 = small_all.reshape(16, 2, 32, SMALL)[:, :, 0, 256:]
+    bf1 = lax.dynamic_index_in_dim(bf1, core, 1, False).reshape(2048).astype(F32)
+    own_cols = lambda v: lax.dynamic_index_in_dim(v.reshape(4, 2, 128), core, 1, False).reshape(512)
+    bias3 = jnp.concatenate([own_cols(bq), jnp.zeros((512,), F32), own_cols(bv)])
+
+    a = toks.astype(F32) + lax.dot_general(
+        picker.astype(BF), small_all[:, :256], (((1,), (1,)), ((), ())), preferred_element_type=F32
+    )
+    n1, hat1, inv1 = layer_norm_forward_pass(a, gain1, shift1)
+    n1b = n1.astype(BF)
+    qkvb = (jnp.dot(n1b, w_qkv, preferred_element_type=F32) + bias3).astype(BF)
+    ob = attend(qkvb, seg)
+    z_part = jnp.dot(ob, w_out, preferred_element_type=F32)
+    z = z_part + swap_halves(swap(z_part.astype(BF), CORE)).astype(F32)
+    a2 = a + z + bo
+    n2, hat2, inv2 = layer_norm_forward_pass(a2, gain2, shift2)
+    n2b = n2.astype(BF)
+    hpre = jnp.dot(n2b, w_up, preferred_element_type=F32) + bf1
+    actb = jax.nn.gelu(hpre, approximate=False).astype(BF)
+    slope = gelu_slope(hpre)
+    dy = gout.astype(F32) * valid
+    dyb = dy.astype(BF)
+    d_down = jnp.einsum("tf,td->fd", actb, dyb, preferred_element_type=F32).astype(BF)
+    down_sum = scatter_xzy(disassemble([d_down], places_down, "xzy", 2048))
+
+    y_part = jnp.dot(actb, w_down, preferred_element_type=F32)
+    y = y_part[:rows] + swap(y_part[rows:].astype(BF), CORE).astype(F32)
+    layer_out = (a2[:rows] + y + bf2).astype(BF)
+
+    dgate = jnp.einsum("td,fd->tf", dyb, w_down, preferred_element_type=F32)
+    dhb = (dgate * slope).astype(BF)
+    d_up = jnp.einsum("td,tf->df", n2b, dhb, preferred_element_type=F32).astype(BF)
+    up_sum = scatter_zxy(disassemble([d_up], places_up, "zxy", 2048))
+    d_up_bias = jnp.sum(dhb.astype(F32), axis=0)
+    dn2_part = jnp.einsum("tf,df->td", dhb, w_up, preferred_element_type=F32)
+    dn2 = dn2_part + swap_halves(swap(dn2_part.astype(BF), CORE)).astype(F32)
+    back2, _, _ = layer_norm_backward_pass(dn2, hat2, inv2, gain2)
+    d_gain2 = jnp.sum(dn2[:rows] * hat2[:rows], axis=0)
+    d_shift2 = jnp.sum(dn2[:rows], axis=0)
+    da2 = dy + back2
+    dzb = da2.astype(BF)
+    d_out_bias = jnp.sum(dzb[:rows].astype(F32), axis=0)
+    d_out = jnp.einsum("te,td->ed", ob, dzb, preferred_element_type=F32).astype(BF)
+    dob = jnp.einsum("td,ed->te", dzb, w_out, preferred_element_type=F32).astype(BF)
+    d_out = d_out.reshape(4, 2, 2, 32, D)
+    mine = lax.dynamic_index_in_dim(d_out, core, 2, False)
+    other = swap(lax.dynamic_index_in_dim(d_out, 1 - core, 2, False), CORE)
+    d_out = jnp.stack(
+        [jnp.where(core == 0, mine, other), jnp.where(core == 0, other, mine)], axis=1
+    ).reshape(16, 32, D)
+
+    dqkvb = jnp.concatenate(attend_back(qkvb, dob, seg), axis=1)
+    d_qkv = jnp.einsum("td,te->de", n1b, dqkvb, preferred_element_type=F32).astype(BF)
+    dqkv_sum = jnp.sum(dqkvb.astype(F32), axis=0)
+    dn1_part = jnp.einsum("te,de->td", dqkvb, w_qkv, preferred_element_type=F32)
+    dn1 = dn1_part[:rows] + swap(dn1_part[rows:].astype(BF), CORE).astype(F32)
+    back1, d_gain1, d_shift1 = layer_norm_backward_pass(dn1, hat1[:rows], inv1[:rows], gain1)
+    da = da2[:rows] + back1
+    tokens_grad = da.astype(BF)
+    d_pos = lax.dot_general(
+        da, picker[:rows].astype(F32), (((0,), (0,)), ((), ())), precision=lax.Precision.HIGHEST
+    )
+    spread = lambda v: jnp.stack(
+        [jnp.where(core == i, v.reshape(4, 128), 0.0) for i in range(2)], axis=1
+    ).reshape(D)
+    d_vec = jnp.stack(
+        [
+            d_gain1,
+            d_shift1,
+            spread(dqkv_sum[:512]),
+            spread(dqkv_sum[1024:]),
+            d_out_bias,
+            d_gain2,
+            d_shift2,
+            jnp.sum(dy[:rows], axis=0),
+        ],
+        axis=1,
+    )
+    d_bias = jnp.where(
+        (jnp.arange(2)[None, :, None, None] == core) & (jnp.arange(32)[None, None, :, None] == 0),
+        d_up_bias.reshape(16, 1, 1, 128),
+        0.0,
+    ).reshape(D, 128)
+    d_small = jnp.concatenate([d_pos[:, :145], d_vec, jnp.zeros((D, 103), F32), d_bias], axis=1).astype(BF)
+    a_sum = scatter_zxy(disassemble([d_small, d_qkv, d_out], places_a, "zxy", A_WIDTH))
+
+    own = jnp.concatenate([a_sum[:32, :cut], up_sum[:32]], axis=1)
+    got = swap(jnp.concatenate([a_sum[32:, :cut], up_sum[32:]], axis=1), CORE)
+    small_own = own[:, :SMALL] + got[:, :SMALL]
+    qkv_grad = weave_blocks(own[:, SMALL:cut], got[:, SMALL:cut], core)
+    up_grad = weave_blocks(own[:, cut:], got[:, cut:], core)
+    out_grad = jnp.concatenate([a_sum[:32, cut:], a_sum[32:, cut:]], axis=1)
+    down_grad = jnp.concatenate([down_sum[:, :D], down_sum[:, D:]])
+    pos_grad = small_own[:, :145].T
+    gv = small_own[:, 145:153].T
+    return (
+        layer_out,
+        tokens_grad,
+        gv[0],
+        gv[1],
+        qkv_grad,
+        gv[2],
+        gv[3],
+        out_grad,
+        gv[4],
+        gv[5],
+        gv[6],
+        up_grad,
+        small_own[0, 256:],
+        down_grad,
+        gv[7],
+        pos_grad,
+    )
+
+
 def solution(mesh):
     in_specs = (
         P(("dp", "fsdp"), None),
@@ -338,6 +839,7 @@
         P(("dp", "fsdp")),
         P(None, ("dp", "fsdp")),
     )
+    eight_by_four = mesh.shape["dp"] == 8 and mesh.shape["fsdp"] == 4
     return jax.shard_map(
-        on_device, mesh=mesh, in_specs=in_specs, out_specs=out_specs, check_vma=False
-    )
+        fast_on_device if eight_by_four else on_device, mesh=mesh, in_specs=in_specs, out_specs=out_specs, check_vma=False
+    )

time: 1540 us -> 515 us (0.33)
  waiting for transfers between devices: 1130 us -> 213 us
  blocking collectives: 159 us -> 0 us
  starting transfers between devices: 0.55 us -> 72.9 us
  matrix products: 135 us -> 68.3 us
  Pallas kernels: 0 us -> 52.1 us
  other arithmetic: 16.2 us -> 32 us
    reduce_scatter x5 -> x0, waiting for transfers between devices: 792 us -> none  [the longest x1 182 us: reduce_grads(): lax.psum_scatter(parts[3], ('dp', 'fsdp'), scatter_dimension=0, tiled=True)]
    all_gather x8 -> x0, waiting for transfers between devices: 254 us -> none  [the longest x2 120 us: fetch(): lax.all_gather(parts[3], ('dp', 'fsdp'), axis=0, tiled=True)]
    ppermute x0 -> x52, waiting for transfers between devices: none -> 213 us  [swap(): return lax.ppermute(value, AXES, [(i, i ^ mask) for i in range(32)])]
    all_gather x3 -> x0, blocking collectives: 120 us -> none  [the longest x1 44.9 us: fetch(): lax.all_gather(parts[6], ('dp', 'fsdp'), axis=1, tiled=True)]
    unnamed x15 -> x0, waiting for transfers between devices: 83.5 us -> none
    ppermute x0 -> x52, starting transfers between devices: none -> 72.9 us  [swap(): return lax.ppermute(value, AXES, [(i, i ^ mask) for i in range(32)])]
    dot_general x42 -> x14, matrix products: 135 us -> 68.3 us  [the longest x1 18.6 us: fast_on_device(): hpre = jnp.dot(n2b, w_up, preferred_element_type=F32) + bf1]
    pallas_call x0 -> x8, Pallas kernels: none -> 52.1 us  [the longest x6 23.7 us: mover(): pl.pallas_call(kernel, out_shape=[jax.ShapeDtypeStruct(s, BF) for s in ou...]
  transfers between devices with their start and end apart: 14 -> 52, of which waited for: 11 -> 17; matrix products, arithmetic and copies ran while one was open for 14% -> 30% of each run, Pallas kernels for 0% -> 10%
where the time goes in v1:
time: 515 us; the launch traced here: 510 us
  waiting for transfers between devices  213 us (41%)
  starting transfers between devices  72.9 us (14%)
  local copies, waits for them, and re-layouts  69.5 us (13%)
  matrix products  68.3 us (13%)
  Pallas kernels  52.1 us (10%)
  other arithmetic  32 us (6%)
    ppermute x52, waiting for transfers between devices, swap(): return lax.ppermute(value, AXES, [(i, i ^ mask) for i in range(32)])  213 us
    ppermute x52, starting transfers between devices, swap(): return lax.ppermute(value, AXES, [(i, i ^ mask) for i in range(32)])  72.9 us
    unnamed x179, local copies, waits for them, and re-layouts  31.4 us
    pallas_call x6, Pallas kernels, mover(): pl.pallas_call(kernel, out_shape=[jax.ShapeDtypeStruct(s, BF) for s in ou...  23.7 us
    dot_general x1, matrix products, fast_on_device(): hpre = jnp.dot(n2b, w_up, preferred_element_type=F32) + bf1  18.6 us
    pallas_call x1, Pallas kernels, attend_back(): pl.pallas_call(attend_back_kernel, grid=(2, 4), in_specs=[part(0), part(4...  18.2 us
    dot_general x1, matrix products, fast_on_device(): dgate = jnp.einsum('td,fd->tf', dyb, w_down, preferred_element_type=F32)  10.6 us
  transfers between devices with their start and end apart: 52, of which 17 were waited for; matrix products, arithmetic and copies ran while one was open for 30% of the time, Pallas kernels for 10%

profile of v1, /device:TPU:0, one launch (start us, length us, event | category | flops | bytes accessed | tf_op | source)
XLA Modules:
  0.0 510.1 jit_solution(5948022651644951695)
XLA Ops:
  35.6 3.7 collective-permute-start.4
  40.0 7.7 %collective-permute-done.4 = bf16[64,2432]{1,0:T(8,128)(2,1)S(1)} collective-permute-done((bf16[64,2432]{1,0:T(8,128)(2,1)S(1)}, bf16[64,2432]{1,0:T(8,128)(2,1)S(1)}, u32[]{:S(2)}, u32[]{:S(2)}) %collective-permute-start.4) | collective-permute-done | bytes 311328 | tf_op jit(solution)/shard_map/ppermute | solution.py:311
  47.7 14.0 %collective-permute-start.12 = (bf16[64,2048]{1,0:T(8,128)(2,1)S(1)}, bf16[64,2048]{1,0:T(8,128)(2,1)S(1)}, u32[]{:S(2)}, u32[]{:S(2)}) collective-permute-start(bf16[64,2048]{1,0:T(8,128)(2,1)S(1)} %pad_maximum_fusion.15), channel_id=1, source_target_pairs={{0,16},{1,17},{2,18},{3,19},{4,20},{5,21},{6,22},{7,23},{8,24},{9,... | collective-permute-start | bytes 786440 | tf_op jit(solution)/shard_map/ppermute | solution.py:311
  61.7 10.7 %collective-permute-done.3 = bf16[64,2432]{1,0:T(8,128)(2,1)S(1)} collective-permute-done((bf16[64,2432]{1,0:T(8,128)(2,1)S(1)}, bf16[64,2432]{1,0:T(8,128)(2,1)S(1)}, u32[]{:S(2)}, u32[]{:S(2)}) %collective-permute-start.3) | collective-permute-done | bytes 311328 | tf_op jit(solution)/shard_map/ppermute | solution.py:311
  76.4 11.7 %collective-permute-done.12 = bf16[64,2048]{1,0:T(8,128)(2,1)S(1)} collective-permute-done((bf16[64,2048]{1,0:T(8,128)(2,1)S(1)}, bf16[64,2048]{1,0:T(8,128)(2,1)S(1)}, u32[]{:S(2)}, u32[]{:S(2)}) %collective-permute-start.12) | collective-permute-done | bytes 262176 | tf_op jit(solution)/shard_map/ppermute | solution.py:311
  90.6 9.4 %collective-permute-done.11 = bf16[64,2048]{1,0:T(8,128)(2,1)S(1)} collective-permute-done((bf16[64,2048]{1,0:T(8,128)(2,1)S(1)}, bf16[64,2048]{1,0:T(8,128)(2,1)S(1)}, u32[]{:S(2)}, u32[]{:S(2)}) %collective-permute-start.11) | collective-permute-done | bytes 262176 | tf_op jit(solution)/shard_map/ppermute | solution.py:311
  100.1 12.8 %collective-permute-start.21 = (bf16[4,32,2048]{2,1,0:T(8,128)(2,1)S(1)}, bf16[4,32,2048]{2,1,0:T(8,128)(2,1)S(1)}, u32[]{:S(2)}, u32[]{:S(2)}) collective-permute-start(bf16[4,32,2048]{2,1,0:T(8,128)(2,1)S(1)} %pad_maximum_fusion.11.refs_0_), channel_id=1, source_target_pairs={{0,16},{1,17},{2,18},{3,19},{4,20},{5,21},{6,22},{7,23},{8,24},{9,... | collective-permute-start | bytes 1572872 | tf_op jit(solution)/shard_map/ppermute | solution.py:311
  114.5 21.6 %collective-permute-done.21.refs_2_ = bf16[4,32,2048]{2,1,0:T(8,128)(2,1)S(1)} collective-permute-done((bf16[4,32,2048]{2,1,0:T(8,128)(2,1)S(1)}, bf16[4,32,2048]{2,1,0:T(8,128)(2,1)S(1)}, u32[]{:S(2)}, u32[]{:S(2)}) %collective-permute-start.21) | collective-permute-done | bytes 524320 | tf_op jit(solution)/shard_map/ppermute | solution.py:311
  138.2 12.9 %collective-permute-done.7.refs_3_ = bf16[2,64,2432]{2,1,0:T(8,128)(2,1)S(1)} collective-permute-done((bf16[2,64,2432]{2,1,0:T(8,128)(2,1)S(1)}, bf16[2,64,2432]{2,1,0:T(8,128)(2,1)S(1)}, u32[]{:S(2)}, u32[]{:S(2)}) %collective-permute-start.7) | collective-permute-done | bytes 622624 | tf_op jit(solution)/shard_map/ppermute | solution.py:311
  151.1 3.5 shard_map.306
  163.9 10.2 %shard_map.307 = bf16[768,512]{1,0:T(8,128)(2,1)S(1)} custom-call(bf16[768,1536]{1,0:T(8,128)(2,1)S(1)} %add_convert_fusion.q_ref.k_ref.v_ref, bf16[768,1536]{1,0:T(8,128)(2,1)S(1)} %add_convert_fusion.q_ref.k_ref.v_ref, bf16[768,1536]{1,0:T(8,128)(2,1)S(1)} %add_convert_fusion.q_ref.k_ref.v_ref, s32[768,1]{1,0:T(8,128)S(1)} %copy-done.12, ...), custom_call_target="tpu_custom_call" | custom-call | flops 1500000000 | bytes 4000000 | tf_op jit(solution)/shard_map/pallas_call | solution.py:561
  189.2 16.3 %collective-permute-done.23.refs_4_ = bf16[4,2,32,2048]{3,2,1,0:T(8,128)(2,1)} collective-permute-done((bf16[4,2,32,2048]{3,2,1,0:T(8,128)(2,1)}, bf16[4,2,32,2048]{3,2,1,0:T(8,128)(2,1)}, u32[]{:S(2)}, u32[]{:S(2)}) %collective-permute-start.23) | collective-permute-done | bytes 1048608 | tf_op jit(solution)/shard_map/ppermute | solution.py:311
  211.3 3.3 shard_map.309
  217.1 4.1 shard_map.308
  225.4 18.6 %fusion.2 = (bf16[768,2048]{1,0:T(8,128)(2,1)S(1)}, f32[768,2048]{1,0:T(8,128)}) fusion(f32[2048]{0:T(1024)S(1)} %bitcast.222, bf16[1024,2048]{1,0:T(8,128)(2,1)S(1)} %shard_map.308, f32[768,1024]{1,0:T(8,128)S(1)} %subtract_multiply_fusion, f32[1024]{0:T(1024)S(1)} %get-tuple-element.63, f32[1024]{0:T(1024)S(1)} %get-tuple-element.64), kind=kOutput, calls=%fused_computation.4 | convolution fusion | flops 3327393792 | bytes 16793600 | tf_op jit(solution)/shard_map/dot_general | solution.py:704
  244.0 3.4 fusion.82
  248.6 10.6 %convert_reduce_fusion = (bf16[2048]{0:T(1024)(128)(2,1)S(1)}, bf16[768,2048]{1,0:T(8,128)(2,1)}) fusion(f32[768,2048]{1,0:T(8,128)} %get-tuple-element.219, f32[2048]{0:T(1024)S(1)} %bitcast.223, bf16[2048,1024]{1,0:T(8,128)(2,1)S(1)} %shard_map.309, f32[768]{0:T(1024)S(1)} %compare_convert_fusion, bf16[384,1024]{1,0:T(8,128)(2,1)S(1)} %collective-permute-done.26, ...), kind=kOutput, calls=%fused_computation.11 | convolution fusion | flops 3246389248 | bytes 15219712 | tf_op jit(solution)/shard_map/td,fd->tf/dot_general | solution.py:716
  259.1 5.6 %convolution_convert_fusion.2.refs_0_ = bf16[1024,2048]{1,0:T(8,128)(2,1)S(1)} fusion(bf16[768,2048]{1,0:T(8,128)(2,1)} %get-tuple-element.223, f32[768,1024]{1,0:T(8,128)S(1)} %subtract_multiply_fusion, f32[1024]{0:T(1024)S(1)} %get-tuple-element.63, f32[1024]{0:T(1024)S(1)} %get-tuple-element.64), kind=kOutput, calls=%fused_computation.31 | convolution fusion | flops 3225681920 | bytes 10493952 | tf_op jit(solution)/shard_map/td,tf->df/dot_general | solution.py:718
  264.7 7.0 %shard_map.312 = (bf16[4,64,2048]{2,1,0:T(8,128)(2,1)S(1)}, bf16[4,64,2048]{2,1,0:T(8,128)(2,1)S(1)}, bf16[4,64,2048]{2,1,0:T(8,128)(2,1)S(1)}, bf16[2,64,2048]{2,1,0:T(8,128)(2,1)S(1)}, bf16[2,64,2048]{2,1,0:T(8,128)(2,1)S(1)}) custom-call(bf16[1024,2048]{1,0:T(8,128)(2,1)S(1)} %convolution_convert_fusion.2.refs_0_), custom_call_target="tpu_custom_call" | custom-call | bytes 8388608 | tf_op jit(solution)/shard_map/pallas_call | solution.py:429
  273.9 4.1 convolution_convert_fusion.1.refs_0_
  283.7 5.3 %fusion.81 = (bf16[768,1024]{1,0:T(8,128)(2,1)S(1)}, f32[768,1024]{1,0:T(8,128)S(1)}) fusion(bf16[768,2048]{1,0:T(8,128)(2,1)} %get-tuple-element.223, bf16[1024,2048]{1,0:T(8,128)(2,1)S(1)} %shard_map.308), kind=kOutput, calls=%fused_computation.387 | convolution fusion | flops 3222011904 | bytes 12058624 | tf_op jit(solution)/shard_map/tf,df->td/dot_general | solution.py:721
  293.1 16.0 %collective-permute-done.45 = bf16[4,2,32,2048]{3,2,1,0:T(8,128)(2,1)S(1)} collective-permute-done((bf16[4,2,32,2048]{3,2,1,0:T(8,128)(2,1)S(1)}, bf16[4,2,32,2048]{3,2,1,0:T(8,128)(2,1)S(1)}, u32[]{:S(2)}, u32[]{:S(2)}) %collective-permute-start.45) | collective-permute-done | bytes 1048608 | tf_op jit(solution)/shard_map/ppermute | solution.py:311
  316.6 3.2 fusion.72
  322.0 18.2 %shard_map.310 = (bf16[768,512]{1,0:T(8,128)(2,1)S(1)}, bf16[768,512]{1,0:T(8,128)(2,1)S(1)}, bf16[768,512]{1,0:T(8,128)(2,1)S(1)}) custom-call(bf16[768,1536]{1,0:T(8,128)(2,1)S(1)} %add_convert_fusion.q_ref.k_ref.v_ref, bf16[768,1536]{1,0:T(8,128)(2,1)S(1)} %add_convert_fusion.q_ref.k_ref.v_ref, bf16[768,1536]{1,0:T(8,128)(2,1)S(1)} %add_convert_fusion.q_ref.k_ref.v_ref, ...), custom_call_target="tpu_custom_call" | custom-call | flops 3000000000 | bytes 6000000 | tf_op jit(solution)/shard_map/pallas_call | solution.py:582
  342.1 4.3 fusion.83
  355.9 6.2 %convolution_convert_fusion.refs_1_ = bf16[1024,1536]{1,0:T(8,128)(2,1)} fusion(bf16[768,1536]{1,0:T(8,128)(2,1)S(1)} %constant_dynamic-update-slice_fusion.58, f32[768,1024]{1,0:T(8,128)} %copy-done.21, f32[1024]{0:T(1024)S(1)} %get-tuple-element.68, f32[1024]{0:T(1024)S(1)} %get-tuple-element.69), kind=kOutput, calls=%fused_computation.29 | convolution fusion | flops 2419851264 | bytes 8658944 | tf_op jit(solution)/shard_map/td,te->de/dot_general | solution.py:739
  384.4 25.3 %collective-permute-done.48 = bf16[4,32,2048]{2,1,0:T(8,128)(2,1)} collective-permute-done((bf16[4,32,2048]{2,1,0:T(8,128)(2,1)}, bf16[4,32,2048]{2,1,0:T(8,128)(2,1)}, u32[]{:S(2)}, u32[]{:S(2)}) %collective-permute-start.48) | collective-permute-done | bytes 524320 | tf_op jit(solution)/shard_map/ppermute | solution.py:311
  414.2 14.6 %collective-permute-done.30 = bf16[2,64,2432]{2,1,0:T(8,128)(2,1)S(1)} collective-permute-done((bf16[2,64,2432]{2,1,0:T(8,128)(2,1)S(1)}, bf16[2,64,2432]{2,1,0:T(8,128)(2,1)S(1)}, u32[]{:S(2)}, u32[]{:S(2)}) %collective-permute-start.30) | collective-permute-done | bytes 622624 | tf_op jit(solution)/shard_map/ppermute | solution.py:311
  434.4 23.3 %collective-permute-done.50 = bf16[32,2048]{1,0:T(8,128)(2,1)S(1)} collective-permute-done((bf16[32,2048]{1,0:T(8,128)(2,1)S(1)}, bf16[32,2048]{1,0:T(8,128)(2,1)S(1)}, u32[]{:S(2)}, u32[]{:S(2)}) %collective-permute-start.50) | collective-permute-done | bytes 131104 | tf_op jit(solution)/shard_map/ppermute | solution.py:311
  464.1 4.6 collective-permute-done.43
  468.7 24.8 %collective-permute-done.42 = bf16[64,2048]{1,0:T(8,128)(2,1)S(1)} collective-permute-done((bf16[64,2048]{1,0:T(8,128)(2,1)S(1)}, bf16[64,2048]{1,0:T(8,128)(2,1)S(1)}, u32[]{:S(2)}, u32[]{:S(2)}) %collective-permute-start.42) | collective-permute-done | bytes 262176 | tf_op jit(solution)/shard_map/ppermute | solution.py:311
  494.8 9.2 %collective-permute-done.35 = bf16[64,2432]{1,0:T(8,128)(2,1)S(1)} collective-permute-done((bf16[64,2432]{1,0:T(8,128)(2,1)S(1)}, bf16[64,2432]{1,0:T(8,128)(2,1)S(1)}, u32[]{:S(2)}, u32[]{:S(2)}) %collective-permute-start.35) | collective-permute-done | bytes 311328 | tf_op jit(solution)/shard_map/ppermute | solution.py:311
  (432 shorter events, 161.2 us)
Async XLA Ops:
  1.8 72.0 %collective-permute-start.18 = (bf16[32,2048]{1,0:T(8,128)(2,1)S(1)}, bf16[32,2048]{1,0:T(8,128)(2,1)S(1)}, u32[]{:S(2)}, u32[]{:S(2)}) collective-permute-start(bf16[32,2048]{1,0:T(8,128)(2,1)S(1)} %get-tuple-element.142), channel_id=1, source_target_pairs={{0,2},{1,3},{2,0},{3,1},{4,6},{5,7},{6,4},{7,5},{8,10},{9,11},{10,... | collective-permute-start | bytes 393224 | tf_op jit(solution)/shard_map/ppermute | solution.py:311
  4.8 69.0 %collective-permute-start.19 = (bf16[32,2048]{1,0:T(8,128)(2,1)S(1)}, bf16[32,2048]{1,0:T(8,128)(2,1)S(1)}, u32[]{:S(2)}, u32[]{:S(2)}) collective-permute-start(bf16[32,2048]{1,0:T(8,128)(2,1)S(1)} %get-tuple-element.143), channel_id=1, source_target_pairs={{0,4},{1,5},{2,6},{3,7},{4,0},{5,1},{6,2},{7,3},{8,12},{9,13},{10,... | collective-permute-start | bytes 393224 | tf_op jit(solution)/shard_map/ppermute | solution.py:311
  39.2 33.2 %collective-permute-start.3 = (bf16[64,2432]{1,0:T(8,128)(2,1)S(1)}, bf16[64,2432]{1,0:T(8,128)(2,1)S(1)}, u32[]{:S(2)}, u32[]{:S(2)}) collective-permute-start(bf16[64,2432]{1,0:T(8,128)(2,1)S(1)} %fusion.52), channel_id=1, source_target_pairs={{0,16},{1,17},{2,18},{3,19},{4,20},{5,21},{6,22},{7,23},{8,24},{9,... | collective-permute-start | bytes 933896 | tf_op jit(solution)/shard_map/ppermute | solution.py:311
  39.2 33.2 %collective-permute-start.2 = (bf16[64,2432]{1,0:T(8,128)(2,1)S(1)}, bf16[64,2432]{1,0:T(8,128)(2,1)S(1)}, u32[]{:S(2)}, u32[]{:S(2)}) collective-permute-start(bf16[64,2432]{1,0:T(8,128)(2,1)S(1)} %fusion.52), channel_id=1, source_target_pairs={{0,8},{1,9},{2,10},{3,11},{4,12},{5,13},{6,14},{7,15},{8,0},{9,1},... | collective-permute-start | bytes 933896 | tf_op jit(solution)/shard_map/ppermute | solution.py:311
  47.7 40.3 %collective-permute-start.12 = (bf16[64,2048]{1,0:T(8,128)(2,1)S(1)}, bf16[64,2048]{1,0:T(8,128)(2,1)S(1)}, u32[]{:S(2)}, u32[]{:S(2)}) collective-permute-start(bf16[64,2048]{1,0:T(8,128)(2,1)S(1)} %pad_maximum_fusion.15), channel_id=1, source_target_pairs={{0,16},{1,17},{2,18},{3,19},{4,20},{5,21},{6,22},{7,23},{8,24},{9,... | collective-permute-start | bytes 786440 | tf_op jit(solution)/shard_map/ppermute | solution.py:311
  72.6 40.6 %collective-permute-start.6 = (bf16[4,64,2432]{2,1,0:T(8,128)(2,1)S(1)}, bf16[4,64,2432]{2,1,0:T(8,128)(2,1)S(1)}, u32[]{:S(2)}, u32[]{:S(2)}) collective-permute-start(bf16[4,64,2432]{2,1,0:T(8,128)(2,1)S(1)} %pad_maximum_fusion.refs_0_), channel_id=1, source_target_pairs={{0,4},{1,5},{2,6},{3,7},{4,0},{5,1},{6,2},{7,3},{8,12},{9,13},{10,... | collective-permute-start | bytes 3735560 | tf_op jit(solution)/shard_map/ppermute | solution.py:311
  73.2 40.6 %collective-permute-start.5 = (bf16[4,64,2432]{2,1,0:T(8,128)(2,1)S(1)}, bf16[4,64,2432]{2,1,0:T(8,128)(2,1)S(1)}, u32[]{:S(2)}, u32[]{:S(2)}) collective-permute-start(bf16[4,64,2432]{2,1,0:T(8,128)(2,1)S(1)} %pad_maximum_fusion.refs_0_), channel_id=1, source_target_pairs={{0,2},{1,3},{2,0},{3,1},{4,6},{5,7},{6,4},{7,5},{8,10},{9,11},{10,... | collective-permute-start | bytes 3735560 | tf_op jit(solution)/shard_map/ppermute | solution.py:311
  73.8 39.3 %collective-permute-start.22 = (bf16[4,32,2048]{2,1,0:T(8,128)(2,1)S(1)}, bf16[4,32,2048]{2,1,0:T(8,128)(2,1)S(1)}, u32[]{:S(2)}, u32[]{:S(2)}) collective-permute-start(bf16[4,32,2048]{2,1,0:T(8,128)(2,1)S(1)} %pad_maximum_fusion.11.refs_0_), channel_id=1, source_target_pairs={{0,24},{1,25},{2,26},{3,27},{4,28},{5,29},{6,30},{7,31},{8,16},{9,... | collective-permute-start | bytes 1572872 | tf_op jit(solution)/shard_map/ppermute | solution.py:311
  100.1 56.9 %collective-permute-start = (bf16[384,1024]{1,0:T(8,128)(2,1)S(1)}, bf16[384,1024]{1,0:T(8,128)(2,1)S(1)}, u32[]{:S(2)}, u32[]{:S(2)}) collective-permute-start(bf16[384,1024]{1,0:T(8,128)(2,1)S(1)} %copy-done.35), channel_id=1, source_target_pairs={{0,1},{1,0},{2,3},{3,2},{4,5},{5,4},{6,7},{7,6},{8,9},{9,8},{10,11... | collective-permute-start | bytes 2359304 | tf_op jit(solution)/shard_map/ppermute | solution.py:311
  100.1 35.9 %collective-permute-start.21 = (bf16[4,32,2048]{2,1,0:T(8,128)(2,1)S(1)}, bf16[4,32,2048]{2,1,0:T(8,128)(2,1)S(1)}, u32[]{:S(2)}, u32[]{:S(2)}) collective-permute-start(bf16[4,32,2048]{2,1,0:T(8,128)(2,1)S(1)} %pad_maximum_fusion.11.refs_0_), channel_id=1, source_target_pairs={{0,16},{1,17},{2,18},{3,19},{4,20},{5,21},{6,22},{7,23},{8,24},{9,... | collective-permute-start | bytes 1572872 | tf_op jit(solution)/shard_map/ppermute | solution.py:311
  113.2 68.4 %collective-permute-start.15 = (bf16[4,64,2048]{2,1,0:T(8,128)(2,1)S(1)}, bf16[4,64,2048]{2,1,0:T(8,128)(2,1)}, u32[]{:S(2)}, u32[]{:S(2)}) collective-permute-start(bf16[4,64,2048]{2,1,0:T(8,128)(2,1)S(1)} %pad_maximum_fusion.4.refs_0_), channel_id=1, source_target_pairs={{0,4},{1,5},{2,6},{3,7},{4,0},{5,1},{6,2},{7,3},{8,12},{9,13},{10,... | collective-permute-start | bytes 3145736 | tf_op jit(solution)/shard_map/ppermute | solution.py:311
  136.8 47.9 %collective-permute-start.14 = (bf16[4,64,2048]{2,1,0:T(8,128)(2,1)S(1)}, bf16[4,64,2048]{2,1,0:T(8,128)(2,1)}, u32[]{:S(2)}, u32[]{:S(2)}) collective-permute-start(bf16[4,64,2048]{2,1,0:T(8,128)(2,1)S(1)} %pad_maximum_fusion.4.refs_0_), channel_id=1, source_target_pairs={{0,2},{1,3},{2,0},{3,1},{4,6},{5,7},{6,4},{7,5},{8,10},{9,11},{10,... | collective-permute-start | bytes 3145736 | tf_op jit(solution)/shard_map/ppermute | solution.py:311
  177.5 44.8 %collective-permute-start.10 = (bf16[768,1024]{1,0:T(8,128)(2,1)}, bf16[768,1024]{1,0:T(8,128)(2,1)}, u32[]{:S(2)}, u32[]{:S(2)}) collective-permute-start(bf16[768,1024]{1,0:T(8,128)(2,1)} %get-tuple-element.216), channel_id=1, source_target_pairs={{0,1},{1,0},{2,3},{3,2},{4,5},{5,4},{6,7},{7,6},{8,9},{9,8},{10,11... | collective-permute-start | bytes 4718600 | tf_op jit(solution)/shard_map/ppermute | solution.py:311
  183.5 33.6 %collective-permute-start.17 = (bf16[2,64,2048]{2,1,0:T(8,128)(2,1)}, bf16[2,64,2048]{2,1,0:T(8,128)(2,1)}, u32[]{:S(2)}, u32[]{:S(2)}) collective-permute-start(bf16[2,64,2048]{2,1,0:T(8,128)(2,1)} %slice.1027), channel_id=1, source_target_pairs={{0,2},{1,3},{2,0},{3,1},{4,6},{5,7},{6,4},{7,5},{8,10},{9,11},{10,... | collective-permute-start | bytes 1572872 | tf_op jit(solution)/shard_map/ppermute | solution.py:311
  186.6 30.5 %collective-permute-start.16 = (bf16[2,64,2048]{2,1,0:T(8,128)(2,1)}, bf16[2,64,2048]{2,1,0:T(8,128)(2,1)}, u32[]{:S(2)}, u32[]{:S(2)}) collective-permute-start(bf16[2,64,2048]{2,1,0:T(8,128)(2,1)} %slice.1026), channel_id=1, source_target_pairs={{0,4},{1,5},{2,6},{3,7},{4,0},{5,1},{6,2},{7,3},{8,12},{9,13},{10,... | collective-permute-start | bytes 1572872 | tf_op jit(solution)/shard_map/ppermute | solution.py:311
  205.5 43.0 %collective-permute-start.26 = (bf16[384,1024]{1,0:T(8,128)(2,1)}, bf16[384,1024]{1,0:T(8,128)(2,1)S(1)}, u32[]{:S(2)}, u32[]{:S(2)}) collective-permute-start(bf16[384,1024]{1,0:T(8,128)(2,1)} %param.20), channel_id=1, source_target_pairs={{0,1},{1,0},{2,3},{3,2},{4,5},{5,4},{6,7},{7,6},{8,9},{9,8},{10,11... | collective-permute-start | bytes 2359304 | tf_op jit(solution)/shard_map/ppermute | solution.py:311
  248.5 130.8 %collective-permute-start.25 = (bf16[384,1024]{1,0:T(8,128)(2,1)}, bf16[384,1024]{1,0:T(8,128)(2,1)}, u32[]{:S(2)}, u32[]{:S(2)}) collective-permute-start(bf16[384,1024]{1,0:T(8,128)(2,1)} %slice.1421), channel_id=1, source_target_pairs={{0,1},{1,0},{2,3},{3,2},{4,5},{5,4},{6,7},{7,6},{8,9},{9,8},{10,11... | collective-permute-start | bytes 2359304 | tf_op jit(solution)/shard_map/ppermute | solution.py:311
  280.7 28.4 %collective-permute-start.45 = (bf16[4,2,32,2048]{3,2,1,0:T(8,128)(2,1)S(1)}, bf16[4,2,32,2048]{3,2,1,0:T(8,128)(2,1)S(1)}, u32[]{:S(2)}, u32[]{:S(2)}) collective-permute-start(bf16[4,2,32,2048]{3,2,1,0:T(8,128)(2,1)S(1)} %get-tuple-element.52), channel_id=1, source_target_pairs={{0,4},{1,5},{2,6},{3,7},{4,0},{5,1},{6,2},{7,3},{8,12},{9,13},{10,... | collective-permute-start | bytes 3145736 | tf_op jit(solution)/shard_map/ppermute | solution.py:311
  281.6 28.3 %collective-permute-start.46 = (bf16[4,2,32,2048]{3,2,1,0:T(8,128)(2,1)S(1)}, bf16[4,2,32,2048]{3,2,1,0:T(8,128)(2,1)S(1)}, u32[]{:S(2)}, u32[]{:S(2)}) collective-permute-start(bf16[4,2,32,2048]{3,2,1,0:T(8,128)(2,1)S(1)} %get-tuple-element.53), channel_id=1, source_target_pairs={{0,2},{1,3},{2,0},{3,1},{4,6},{5,7},{6,4},{7,5},{8,10},{9,11},{10,... | collective-permute-start | bytes 3145736 | tf_op jit(solution)/shard_map/ppermute | solution.py:311
  290.3 141.0 %collective-permute-start.40 = (bf16[4,64,2048]{2,1,0:T(8,128)(2,1)}, bf16[4,64,2048]{2,1,0:T(8,128)(2,1)}, u32[]{:S(2)}, u32[]{:S(2)}) collective-permute-start(bf16[4,64,2048]{2,1,0:T(8,128)(2,1)} %pad_maximum_fusion.9), channel_id=1, source_target_pairs={{0,4},{1,5},{2,6},{3,7},{4,0},{5,1},{6,2},{7,3},{8,12},{9,13},{10,... | collective-permute-start | bytes 3145736 | tf_op jit(solution)/shard_map/ppermute | solution.py:311
  312.3 70.9 %collective-permute-start.47 = (bf16[4,32,2048]{2,1,0:T(8,128)(2,1)}, bf16[4,32,2048]{2,1,0:T(8,128)(2,1)}, u32[]{:S(2)}, u32[]{:S(2)}) collective-permute-start(bf16[4,32,2048]{2,1,0:T(8,128)(2,1)} %get-tuple-element.108), channel_id=1, source_target_pairs={{0,8},{1,9},{2,10},{3,11},{4,12},{5,13},{6,14},{7,15},{8,0},{9,1},... | collective-permute-start | bytes 1572872 | tf_op jit(solution)/shard_map/ppermute | solution.py:311
  364.7 45.0 %collective-permute-start.48 = (bf16[4,32,2048]{2,1,0:T(8,128)(2,1)}, bf16[4,32,2048]{2,1,0:T(8,128)(2,1)}, u32[]{:S(2)}, u32[]{:S(2)}) collective-permute-start(bf16[4,32,2048]{2,1,0:T(8,128)(2,1)} %get-tuple-element.110), channel_id=1, source_target_pairs={{0,16},{1,17},{2,18},{3,19},{4,20},{5,21},{6,22},{7,23},{8,24},{9,... | collective-permute-start | bytes 1572872 | tf_op jit(solution)/shard_map/ppermute | solution.py:311
  379.4 34.0 %collective-permute-start.32 = (bf16[2,64,2432]{2,1,0:T(8,128)(2,1)S(1)}, bf16[2,64,2432]{2,1,0:T(8,128)(2,1)S(1)}, u32[]{:S(2)}, u32[]{:S(2)}) collective-permute-start(bf16[2,64,2432]{2,1,0:T(8,128)(2,1)S(1)} %get-tuple-element.45), channel_id=1, source_target_pairs={{0,2},{1,3},{2,0},{3,1},{4,6},{5,7},{6,4},{7,5},{8,10},{9,11},{10,... | collective-permute-start | bytes 1867784 | tf_op jit(solution)/shard_map/ppermute | solution.py:311
  383.2 49.6 %collective-permute-start.38 = (bf16[4,64,2048]{2,1,0:T(8,128)(2,1)S(1)}, bf16[4,64,2048]{2,1,0:T(8,128)(2,1)S(1)}, u32[]{:S(2)}, u32[]{:S(2)}) collective-permute-start(bf16[4,64,2048]{2,1,0:T(8,128)(2,1)S(1)} %copy-done.29), channel_id=1, source_target_pairs={{0,2},{1,3},{2,0},{3,1},{4,6},{5,7},{6,4},{7,5},{8,10},{9,11},{10,... | collective-permute-start | bytes 3145736 | tf_op jit(solution)/shard_map/ppermute | solution.py:311
  413.7 45.5 %collective-permute-start.33 = (bf16[4,64,2432]{2,1,0:T(8,128)(2,1)S(1)}, bf16[4,64,2432]{2,1,0:T(8,128)(2,1)S(1)}, u32[]{:S(2)}, u32[]{:S(2)}) collective-permute-start(bf16[4,64,2432]{2,1,0:T(8,128)(2,1)S(1)} %pad_maximum_fusion.2), channel_id=1, source_target_pairs={{0,4},{1,5},{2,6},{3,7},{4,0},{5,1},{6,2},{7,3},{8,12},{9,13},{10,... | collective-permute-start | bytes 3735560 | tf_op jit(solution)/shard_map/ppermute | solution.py:311
  429.1 30.1 %collective-permute-start.31 = (bf16[4,64,2432]{2,1,0:T(8,128)(2,1)S(1)}, bf16[4,64,2432]{2,1,0:T(8,128)(2,1)S(1)}, u32[]{:S(2)}, u32[]{:S(2)}) collective-permute-start(bf16[4,64,2432]{2,1,0:T(8,128)(2,1)S(1)} %pad_maximum_fusion.1), channel_id=1, source_target_pairs={{0,2},{1,3},{2,0},{3,1},{4,6},{5,7},{6,4},{7,5},{8,10},{9,11},{10,... | collective-permute-start | bytes 3735560 | tf_op jit(solution)/shard_map/ppermute | solution.py:311
  431.3 27.9 %collective-permute-start.51 = (bf16[32,2048]{1,0:T(8,128)(2,1)S(1)}, bf16[32,2048]{1,0:T(8,128)(2,1)S(1)}, u32[]{:S(2)}, u32[]{:S(2)}) collective-permute-start(bf16[32,2048]{1,0:T(8,128)(2,1)S(1)} %get-tuple-element.135), channel_id=1, source_target_pairs={{0,4},{1,5},{2,6},{3,7},{4,0},{5,1},{6,2},{7,3},{8,12},{9,13},{10,... | collective-permute-start | bytes 393224 | tf_op jit(solution)/shard_map/ppermute | solution.py:311
  434.3 29.7 %collective-permute-start.41 = (bf16[64,2048]{1,0:T(8,128)(2,1)S(1)}, bf16[64,2048]{1,0:T(8,128)(2,1)S(1)}, u32[]{:S(2)}, u32[]{:S(2)}) collective-permute-start(bf16[64,2048]{1,0:T(8,128)(2,1)S(1)} %get-tuple-element.105), channel_id=1, source_target_pairs={{0,8},{1,9},{2,10},{3,11},{4,12},{5,13},{6,14},{7,15},{8,0},{9,1},... | collective-permute-start | bytes 786440 | tf_op jit(solution)/shard_map/ppermute | solution.py:311
  459.2 34.4 %collective-permute-start.42 = (bf16[64,2048]{1,0:T(8,128)(2,1)S(1)}, bf16[64,2048]{1,0:T(8,128)(2,1)S(1)}, u32[]{:S(2)}, u32[]{:S(2)}) collective-permute-start(bf16[64,2048]{1,0:T(8,128)(2,1)S(1)} %get-tuple-element.107), channel_id=1, source_target_pairs={{0,16},{1,17},{2,18},{3,19},{4,20},{5,21},{6,22},{7,23},{8,24},{9,... | collective-permute-start | bytes 786440 | tf_op jit(solution)/shard_map/ppermute | solution.py:311
  459.6 35.1 %collective-permute-start.34 = (bf16[64,2432]{1,0:T(8,128)(2,1)S(1)}, bf16[64,2432]{1,0:T(8,128)(2,1)S(1)}, u32[]{:S(2)}, u32[]{:S(2)}) collective-permute-start(bf16[64,2432]{1,0:T(8,128)(2,1)S(1)} %get-tuple-element.102), channel_id=1, source_target_pairs={{0,8},{1,9},{2,10},{3,11},{4,12},{5,13},{6,14},{7,15},{8,0},{9,1},... | collective-permute-start | bytes 933896 | tf_op jit(solution)/shard_map/ppermute | solution.py:311
  462.6 32.2 %collective-permute-start.36 = (bf16[64,2432]{1,0:T(8,128)(2,1)S(1)}, bf16[64,2432]{1,0:T(8,128)(2,1)S(1)}, u32[]{:S(2)}, u32[]{:S(2)}) collective-permute-start(bf16[64,2432]{1,0:T(8,128)(2,1)S(1)} %get-tuple-element.103), channel_id=1, source_target_pairs={{0,24},{1,25},{2,26},{3,27},{4,28},{5,29},{6,30},{7,31},{8,16},{9,... | collective-permute-start | bytes 933896 | tf_op jit(solution)/shard_map/ppermute | solution.py:311
  464.1 39.9 %collective-permute-start.35 = (bf16[64,2432]{1,0:T(8,128)(2,1)S(1)}, bf16[64,2432]{1,0:T(8,128)(2,1)S(1)}, u32[]{:S(2)}, u32[]{:S(2)}) collective-permute-start(bf16[64,2432]{1,0:T(8,128)(2,1)S(1)} %get-tuple-element.104), channel_id=1, source_target_pairs={{0,16},{1,17},{2,18},{3,19},{4,20},{5,21},{6,22},{7,23},{8,24},{9,... | collective-permute-start | bytes 933896 | tf_op jit(solution)/shard_map/ppermute | solution.py:311
  (69 other events, 1047.8 us)
